TPU v7x, 128 devices: a whole 4x4x4 slice. The times are simulated.
128 devices in a mesh: seg: 16 (over y_lo, x, core), chan: 8 (over y_hi, z).
Axes of the slice: x: 4, y: 4 (y_hi: 2, y_lo: 2; y = y_hi * 2 + y_lo), z: 4, core: 2. Of those that a mesh axis runs over, the one named last changes fastest.
Arguments:
- signal: bfloat16 [256, 256, 2048], P('seg', 'chan'), may hold values from -6 to 6
- latent_factor: float32 [512, 256], replicated, may hold values from -0.375 to 0.375
Outputs:
- smoothed: float32 [512, 256, 2, 256], P(None, ('seg', 'chan'))
All inputs are finite; a program needn't handle non-finite values.
Results may differ from a plain program's by a relative error of at most 0.02.
Values may be sent and summed in bfloat16 or wider, within the bound.
A program may use at most 128 MiB of HBM per device.

v0:
```python
import math

import jax
import jax.numpy as jnp
from jax import lax
from jax.sharding import PartitionSpec as P


def dft_table(length, bins):
    times = jnp.arange(length, dtype=jnp.int32)
    freqs = jnp.arange(bins, dtype=jnp.int32)
    phase = times[:, None] * freqs[None, :] % length
    theta = 2.0 * math.pi * phase.astype(jnp.float32) / length
    window = 0.5 - 0.5 * jnp.cos(2.0 * math.pi * times.astype(jnp.float32) / length)
    weight = window / jnp.sqrt(jnp.float32(3.0 * length / 8.0))
    cos_part = weight[:, None] * jnp.cos(theta)
    sin_part = -weight[:, None] * jnp.sin(theta)
    return jnp.stack([cos_part, sin_part], axis=1).astype(jnp.bfloat16)


def cross_terms(spectra, segs):
    real_part = spectra[:, :, 0, :]
    imag_part = spectra[:, :, 1, :]
    same = jnp.einsum(
        "fsc,fsd->fcd", real_part, real_part, preferred_element_type=jnp.float32
    ) + jnp.einsum("fsc,fsd->fcd", imag_part, imag_part, preferred_element_type=jnp.float32)
    twist = jnp.einsum(
        "fsc,fsd->fcd", real_part, imag_part, preferred_element_type=jnp.float32
    ) - jnp.einsum("fsc,fsd->fcd", imag_part, real_part, preferred_element_type=jnp.float32)
    return jnp.stack([same, twist], axis=2) * (1.0 / segs)


def per_device(signal, latent_factor):
    seg_count, chan_local, length = signal.shape
    bins, rank = latent_factor.shape
    n_seg = lax.axis_size("seg")
    n_chan = lax.axis_size("chan")
    segs = seg_count * n_seg
    table = dft_table(length, bins)
    spectra = jnp.einsum("scl,lkf->fskc", signal, table, preferred_element_type=jnp.float32).astype(
        jnp.bfloat16
    )
    block_bins = bins // (n_seg * n_chan)
    banded = lax.all_to_all(spectra, "chan", split_axis=0, concat_axis=3, tiled=True)
    owned = lax.psum_scatter(
        cross_terms(banded, segs).astype(jnp.bfloat16), "seg", scatter_dimension=0, tiled=True
    ).astype(jnp.float32)
    pairs = lax.all_to_all(
        owned.astype(jnp.bfloat16), ("seg", "chan"), split_axis=1, concat_axis=0, tiled=True
    ).astype(owned.dtype)
    ordered = latent_factor.reshape(n_chan, n_seg, block_bins, rank)
    ordered = jnp.transpose(ordered, (1, 0, 2, 3)).reshape(bins, rank)
    latent = jnp.einsum("fr,fckd->rckd", ordered, pairs, precision=lax.Precision.HIGHEST)
    return jnp.einsum("fr,rckd->fckd", latent_factor, latent, precision=lax.Precision.HIGHEST)


def solution(mesh):
    in_specs = (P("seg", "chan", None), P())
    out_specs = P(None, ("seg", "chan"), None, None)
    return jax.shard_map(
        per_device, mesh=mesh, in_specs=in_specs, out_specs=out_specs, check_vma=False
    )
```

profile of v0, /device:TPU:1, one launch (start us, length us, event | category | flops | bytes accessed | tf_op | source)
XLA Modules:
  0.0 369.4 jit_solution(232264247619098032)
XLA Ops:
  6.5 0.0 copy-start
  6.5 0.0 all-reduce.3.cloned.1.call-start
  6.5 0.1 fusion.28
  6.6 0.1 subtract_multiply_fusion
  6.7 17.7 %multiply_convert_fusion = (bf16[2048,1,512]{2,0,1:T(8,128)(2,1)S(1)}, bf16[2048,1,512]{2,0,1:T(8,128)(2,1)S(1)}) fusion(f32[2048]{0:T(1024)S(1)} %fusion.28, f32[2048]{0:T(1024)S(1)} %subtract_multiply_fusion), kind=kLoop, calls=%fused_computation.14 | loop fusion | flops 18874368 | bytes 4210688 | tf_op jit(solution)/shard_map/convert.1
  24.4 0.0 copy-done
  24.4 2.3 fusion.14
  26.7 6.5 %copy.11 = bf16[512,16,2,32]{3,1,2,0:T(8,128)(2,1)} copy(bf16[512,16,2,32]{0,3,1,2:T(8,128)(2,1)S(1)} %fusion.14) | data formatting | bytes 2097152 | tf_op jit(solution)/shard_map/convert_element_type | solution.py:40
  33.2 7.0 %reshape.137 = bf16[8,2,32768]{2,1,0:T(2,128)(2,1)S(1)} reshape(bf16[512,2,16,32]{3,2,1,0:T(8,128)(2,1)} %bitcast.71) | data formatting | bytes 2097152
  40.1 23.9 %all_to_all.36 = bf16[8,2,32768]{2,1,0:T(2,128)(2,1)S(1)} all-to-all(bf16[8,2,32768]{2,1,0:T(2,128)(2,1)S(1)} %reshape.137), channel_id=1, replica_groups=mesh['seg'=16,'chan'=8] {'chan'}, dimensions={0} | all-to-all | bytes 2097152 | tf_op jit(solution)/shard_map/all_to_all | solution.py:44
  64.0 4.5 %reshape.138 = bf16[512,2,16,32]{3,2,1,0:T(8,128)(2,1)} reshape(bf16[8,2,32768]{2,1,0:T(2,128)(2,1)S(1)} %all_to_all.36) | data formatting | bytes 2097152
  68.5 4.6 %copy.12 = bf16[8,64,16,2,32]{1,4,0,3,2:T(8,128)(2,1)S(1)} copy(bf16[8,64,16,2,32]{4,2,3,1,0:T(8,128)(2,1)} %bitcast.72) | data formatting | bytes 2097152 | tf_op jit(solution)/shard_map/all_to_all | solution.py:44
  73.1 1.2 fusion.30
  74.3 1.9 copy.25
  76.2 0.8 copy.26
  77.1 8.1 %fusion.26 = f32[64,256,256]{2,1,0:T(8,128)} fusion(bf16[64,16,1,256]{3,1,0,2:T(8,128)(2,1)S(1)} %copy.25), kind=kOutput, calls=%fused_computation.33 | convolution fusion | flops 134217728 | bytes 17301504 | tf_op jit(solution)/shard_map/fsc,fsd->fcd/dot_general | solution.py:24
  85.2 8.1 %fusion.21 = f32[64,256,256]{2,1,0:T(8,128)} fusion(bf16[64,16,1,256]{3,1,0,2:T(8,128)(2,1)S(1)} %copy.26, bf16[64,16,1,256]{3,1,0,2:T(8,128)(2,1)S(1)} %copy.25), kind=kOutput, calls=%fused_computation.28 | convolution fusion | flops 134217728 | bytes 17825792 | tf_op jit(solution)/shard_map/fsc,fsd->fcd/dot_general | solution.py:27
  93.3 8.1 %subtract_bitcast_fusion = f32[64,256,1,256]{3,1,0,2:T(8,128)S(1)} fusion(f32[64,256,256]{2,1,0:T(8,128)} %fusion.21, bf16[64,16,1,256]{3,1,0,2:T(8,128)(2,1)S(1)} %copy.26, bf16[64,16,1,256]{3,1,0,2:T(8,128)(2,1)S(1)} %copy.25), kind=kOutput, calls=%fused_computation.2 | convolution fusion | flops 138412032 | bytes 34603008 | tf_op jit(solution)/shard_map/fsc,fsd->fcd/dot_general | solution.py:29
  101.4 13.9 %add_bitcast_fusion = f32[64,256,1,256]{3,1,0,2:T(8,128)} fusion(f32[64,256,256]{2,1,0:T(8,128)} %fusion.26, bf16[64,16,1,256]{3,1,0,2:T(8,128)(2,1)S(1)} %copy.26), kind=kOutput, calls=%fused_computation.3 | convolution fusion | flops 138412032 | bytes 34078720 | tf_op jit(solution)/shard_map/fsc,fsd->fcd/dot_general | solution.py:26
  115.3 15.1 %fusion = bf16[64,256,2,256]{3,1,0,2:T(8,128)(2,1)} fusion(f32[64,256,1,256]{3,1,0,2:T(8,128)S(1)} %subtract_bitcast_fusion, f32[64,256,1,256]{3,1,0,2:T(8,128)} %add_bitcast_fusion), kind=kLoop, calls=%fused_computation.1 | loop fusion | flops 25165824 | bytes 50331648 | tf_op jit(solution)/shard_map/convert_element_type | solution.py:46
  130.4 0.0 copy-start.3
  130.4 0.0 all-reduce.3.cloned.1.call-update
  130.4 0.0 copy-start.2
  130.4 0.6 copy-done.3
  131.0 0.6 dynamic-slice
  132.3 191.7 %all-reduce.3.cloned.1.call-done = bf16[64,256,2,256]{3,1,0,2:T(8,128)(2,1)} async-done(((bf16[64,256,2,256]{3,1,0,2:T(8,128)(2,1)}), bf16[64,256,2,256]{3,1,0,2:T(8,128)(2,1)}) %all-reduce.3.cloned.1.call-update) | async-done | bytes 16777232
  324.0 1.3 constant_dynamic-slice_fusion
  325.3 1.8 copy.15
  327.1 8.4 %all-to-all-start.1 = ((bf16[4,256,2,256]{3,0,2,1:T(4,128)(2,1)}), bf16[4,256,2,256]{3,0,2,1:T(4,128)(2,1)S(1)}, u32[]{:S(2)}, u32[]{:S(2)}) async-start(bf16[4,256,2,256]{3,0,2,1:T(4,128)(2,1)} %copy.15), calls=%async_computation.1 | async-start | bytes 2097152 | tf_op jit(solution)/shard_map/all_to_all | solution.py:48
  335.5 0.0 copy-done.2
  335.5 0.1 reshape.127
  335.7 0.2 reshape.131
  335.9 17.3 %all-to-all-done.1 = bf16[4,256,2,256]{3,0,2,1:T(4,128)(2,1)S(1)} async-done(((bf16[4,256,2,256]{3,0,2,1:T(4,128)(2,1)}), bf16[4,256,2,256]{3,0,2,1:T(4,128)(2,1)S(1)}, u32[]{:S(2)}, u32[]{:S(2)}) %all-to-all-start.1) | async-done | bytes 1048608 | tf_op jit(solution)/shard_map/all_to_all | solution.py:48
  353.2 0.8 copy.16
  354.1 0.0 copy-start.1
  354.1 1.2 convolution_bitcast_fusion.1
  355.3 3.2 convolution_bitcast_fusion
  358.5 4.1 %copy.19 = f32[512,2,2,256]{3,2,1,0:T(2,128)} copy(f32[512,2,2,256]{0,3,2,1:T(8,128)} %convolution_bitcast_fusion) | data formatting | bytes 4194304 | tf_op jit(solution)/shard_map/fr,rckd->fckd/dot_general | solution.py:54
  362.6 0.0 copy-done.1
  (1 shorter events, 0.0 us)
Async XLA Ops:
  6.5 17.8 %copy-start = (bf16[16,32,2048]{2,1,0:T(8,128)(2,1)S(1)}, bf16[16,32,2048]{2,1,0:T(8,128)(2,1)}, u32[]{:S(2)}) copy-start(bf16[16,32,2048]{2,1,0:T(8,128)(2,1)} %param.2) | copy-start | bytes 6291460
  6.5 317.5 %all-reduce.3.cloned.1.call-start = ((), (), s32[]{:S(2)}) async-start(), calls=%async_computation.2 | async-start | bytes 33554432
  130.4 0.7 copy-start.3
  130.4 205.1 %copy-start.2 = (f32[512,256]{1,0:T(8,128)S(1)}, f32[512,256]{1,0:T(8,128)}, u32[]{:S(2)}) copy-start(f32[512,256]{1,0:T(8,128)} %param.3) | copy-start | bytes 1572868
  327.1 26.1 %all-to-all-start.1 = ((bf16[4,256,2,256]{3,0,2,1:T(4,128)(2,1)}), bf16[4,256,2,256]{3,0,2,1:T(4,128)(2,1)S(1)}, u32[]{:S(2)}, u32[]{:S(2)}) async-start(bf16[4,256,2,256]{3,0,2,1:T(4,128)(2,1)} %copy.15), calls=%async_computation.1 | async-start | bytes 2097152 | tf_op jit(solution)/shard_map/all_to_all | solution.py:48
  354.1 8.5 %copy-start.1 = (bf16[16,32,2048]{2,1,0:T(8,128)(2,1)S(1)}, bf16[16,32,2048]{2,1,0:T(8,128)(2,1)}, u32[]{:S(2)}) copy-start(bf16[16,32,2048]{2,1,0:T(8,128)(2,1)} %param.2) | copy-start | bytes 6291460
Sparse Core Ops, SparseCore 0:
  130.5 193.4 all-reduce.2
where the time goes:
time: 370 us; the launch traced here: 369 us
  waiting for transfers between devices  209 us (56%)
  matrix products  45 us (12%)
  local copies, waits for them, and re-layouts  36 us (10%)
  other arithmetic  32.9 us (9%)
  blocking collectives  23.9 us (6%)
  between operations  14.2 us (4%)
  starting transfers between devices  8.41 us (2%)
    unnamed x2, waiting for transfers between devices  192 us
    all_to_all x1, blocking collectives, per_device(): lax.all_to_all(spectra, 'chan', split_axis=0, concat_axis=3, tiled=True)  23.9 us
    another operation x1, other arithmetic  17.7 us
    all_to_all x1, waiting for transfers between devices, per_device(): lax.all_to_all(owned.astype(jnp.bfloat16), ('seg', 'chan'), split_axis=1,...  17.3 us
    unnamed x14, local copies, waits for them, and re-layouts  16.7 us
    convert_element_type x1, other arithmetic, per_device(): cross_terms(banded, segs).astype(jnp.bfloat16)  15.1 us
    dot_general x1, matrix products, cross_terms(): jnp.einsum('fsc,fsd->fcd', imag_part, imag_part, preferred_element_type=j...  13.9 us
    all_to_all x1, starting transfers between devices, per_device(): lax.all_to_all(owned.astype(jnp.bfloat16), ('seg', 'chan'), split_axis=1,...  8.4 us
  transfers between devices with their start and end apart: 2, of which 2 were waited for; matrix products, arithmetic and copies ran while one was open for 0% of the time, Pallas kernels for 0%

commit v1 on v0

v1 whole, which is shorter than its diff:
```python
import functools

import jax
import jax.numpy as jnp
import ml_dtypes
import numpy as np
from jax import lax
from jax.experimental import pallas as pl
from jax.experimental.pallas import tpu as pltpu
from jax.sharding import PartitionSpec as P

MESH = pl.DeviceIdType.MESH
HALVES = 2
NT = (((1,), (1,)), ((), ()))


def dft_rows(length, bins, devices):
    per_half = bins // devices // HALVES
    half, owner, at = np.meshgrid(
        np.arange(HALVES), np.arange(devices), np.arange(per_half), indexing="ij"
    )
    freqs = ((half * per_half + at) * devices + owner).reshape(-1)
    times = np.arange(length)
    theta = 2.0 * np.pi * (freqs[:, None] * times[None, :] % length) / length
    weight = (0.5 - 0.5 * np.cos(2.0 * np.pi * times / length)) / np.sqrt(3.0 * length / 8.0)
    rows = np.stack([weight * np.cos(theta), -weight * np.sin(theta)], axis=1)
    return rows.reshape(-1, length).astype(np.float32).astype(ml_dtypes.bfloat16)


def kernel(
    n_seg, n_chan, segs,
    sig_hbm, tab_hbm, lat_hbm, out_ref,
    sig, tab, lat, send1, recv1, send2, recv2, z, scr, m_hi, m_lo, acc,
    in_sem, send_sem, recv_sem,
):
    n = n_seg * n_chan
    seg, chan = lax.axis_index("seg"), lax.axis_index("chan")
    me = seg * n_chan + chan
    slot = chan * n_seg + seg
    half_rows = tab.shape[0] // HALVES
    bins = m_hi.shape[0]

    sig_in = pltpu.make_async_copy(sig_hbm, sig, in_sem.at[0])
    sig_in.start()
    tab_in = []
    for h in range(HALVES):
        rows = pl.ds(h * half_rows, half_rows)
        tab_in.append(pltpu.make_async_copy(tab_hbm.at[rows], tab.at[rows], in_sem.at[1 + h]))
        tab_in[-1].start()
    lat_in = pltpu.make_async_copy(lat_hbm, lat, in_sem.at[3])
    lat_in.start()

    def coords(d):
        return lax.div(d, n_chan), lax.rem(d, n_chan)

    barrier = pltpu.get_barrier_semaphore()

    def greet(s, carry):
        pl.semaphore_signal(
            barrier, inc=1, device_id=coords(lax.rem(me + s, n)), device_id_type=MESH
        )
        return carry

    lax.fori_loop(1, n, greet, 0)

    def transform(h):
        step = 128
        low = lax.broadcasted_iota(jnp.int32, (step, 128), 0) % 8 < 4

        def block(i, carry):
            rows = pl.ds(pl.multiple_of(h * half_rows + i * step, step), step)
            y = lax.dot_general(tab[rows, :], sig[...], NT, preferred_element_type=jnp.float32)
            v = [y[:, q * 128 : (q + 1) * 128] for q in range(4)]
            up = [pltpu.roll(a, 4, 0) for a in v]
            even = [jnp.where(low, v[q], up[q + 1]) for q in (0, 2)]
            down = [pltpu.roll(a, step - 4, 0) for a in v]
            odd = [jnp.where(low, down[q], v[q + 1]) for q in (0, 2)]
            pairs = step // 8
            both = [
                jnp.concatenate([a.reshape(pairs, 1, 8, 128) for a in part], axis=2)
                for part in (even, odd)
            ]
            block = jnp.concatenate(both, axis=1).reshape(2 * pairs, 16, 128)
            send1[h, pl.ds(i * 2 * pairs, 2 * pairs)] = block.astype(jnp.bfloat16)
            return carry

        lax.fori_loop(0, half_rows // step, block, 0)

    def send(k, src, dst, at):
        def one(s, carry):
            d = lax.rem(me + s, n)
            pltpu.make_async_remote_copy(
                src_ref=src.at[d], dst_ref=dst.at[at], send_sem=send_sem.at[k],
                recv_sem=recv_sem.at[k], device_id=coords(d), device_id_type=MESH,
            ).start()
            return carry

        lax.fori_loop(1, n, one, 0)
        pltpu.make_async_copy(src.at[me], dst.at[at], recv_sem.at[k]).start()

    def arrived(k, src, dst):
        pltpu.make_async_copy(src, dst, recv_sem.at[k]).wait()

    def cross(h):
        width = n_seg * 16
        for j in range(n_chan):
            t = recv1[h, j * n_seg : (j + 1) * n_seg].reshape(width, 128).T
            for s in range(4):
                z[j * 32 : (j + 1) * 32, s * width : (s + 1) * width] = t[s * 32 : (s + 1) * 32]
        zf = z[...].astype(jnp.float32)
        lane = lax.broadcasted_iota(jnp.int32, zf.shape, 1) % 4
        last = zf.shape[1] - 1
        y = jnp.where(lane % 2 == 0, pltpu.roll(zf, last, 1), -pltpu.roll(zf, 1, 1))
        for b in range(2):
            own = lane // 2 == b
            for k, part in enumerate((zf, y)):
                right = jnp.where(own, part, 0.0).astype(jnp.bfloat16)
                c = lax.dot_general(z[...], right, NT, preferred_element_type=jnp.float32)
                for dh in range(2):
                    at = b * 4 + k * 2 + dh
                    scr[pl.ds(at, c.shape[0], stride=8), :] = c[:, dh * 128 : (dh + 1) * 128]
        send2[h] = scr[...].reshape(n, 16, 128).astype(jnp.bfloat16)

    def smooth(h):
        scr[...] = recv2[h].reshape(n * 16, 128).astype(jnp.float32)
        left = pl.ds(h * 2 * n, 2 * n)
        for c in range(2):
            for dh in range(2):
                for k in range(2):
                    at = c * 4 + dh * 2 + k
                    x = jnp.concatenate(
                        [
                            scr[pl.ds(c * 8 + b * 4 + k * 2 + dh, n, stride=16), :]
                            for b in range(2)
                        ],
                        axis=0,
                    ).astype(jnp.bfloat16)
                    r = jnp.dot(m_hi[:, left], x, preferred_element_type=jnp.float32)
                    r = r + jnp.dot(m_lo[:, left], x, preferred_element_type=jnp.float32)
                    if h == 0:
                        acc[at] = r
                    else:
                        out_ref[pl.ds(at, bins, stride=8), :] = r + acc[at]

    sig_in.wait()
    tab_in[0].wait()
    transform(0)
    pl.semaphore_wait(barrier, n - 1)
    send(0, send1.at[0], recv1.at[0], slot)
    tab_in[1].wait()
    transform(1)
    send(1, send1.at[1], recv1.at[1], slot)
    lat_in.wait()
    m = lax.dot_general(
        lat[...], lat[...], NT, preferred_element_type=jnp.float32, precision=lax.Precision.HIGHEST
    ) * (1.0 / segs)
    m_hi[...] = m.astype(jnp.bfloat16)
    m_lo[...] = (m - m_hi[...].astype(jnp.float32)).astype(jnp.bfloat16)
    for h in range(HALVES):
        arrived(h, send1.at[h], recv1.at[h])
        cross(h)
        send(2 + h, send2.at[h], recv2.at[h], me)
    for h in range(HALVES):
        arrived(2 + h, send2.at[h], recv2.at[h])
        smooth(h)
    for k in range(2 * HALVES):
        src = (send1, send2)[k // HALVES].at[k % HALVES, pl.ds(0, n - 1)]
        pltpu.make_async_copy(src, src, send_sem.at[k]).wait()


def per_device(signal, latent_factor):
    seg_count, chan_local, length = signal.shape
    bins, rank = latent_factor.shape
    n_seg = lax.axis_size("seg")
    n_chan = lax.axis_size("chan")
    n = n_seg * n_chan
    channels = chan_local * n_chan
    table = jnp.asarray(dft_rows(length, bins, n))
    bf16, f32 = jnp.bfloat16, jnp.float32
    out = pl.pallas_call(
        functools.partial(kernel, n_seg, n_chan, seg_count * n_seg),
        out_shape=jax.ShapeDtypeStruct((bins * 8, 128), f32),
        in_specs=[pl.BlockSpec(memory_space=pl.ANY)] * 3,
        out_specs=pl.BlockSpec(memory_space=pltpu.VMEM),
        scratch_shapes=[
            pltpu.VMEM((seg_count * chan_local, length), bf16),
            pltpu.VMEM(table.shape, bf16),
            pltpu.VMEM((bins, rank), f32),
            pltpu.VMEM((HALVES, n, 16, 128), bf16),
            pltpu.VMEM((HALVES, n, 16, 128), bf16),
            pltpu.VMEM((HALVES, n, 16, 128), bf16),
            pltpu.VMEM((HALVES, n, 16, 128), bf16),
            pltpu.VMEM((channels, 64 * n_seg), bf16),
            pltpu.VMEM((n * 16, 128), f32),
            pltpu.VMEM((bins, bins), bf16),
            pltpu.VMEM((bins, bins), bf16),
            pltpu.VMEM((8, bins, 128), f32),
            pltpu.SemaphoreType.DMA((4,)),
            pltpu.SemaphoreType.DMA((2 * HALVES,)),
            pltpu.SemaphoreType.DMA((2 * HALVES,)),
        ],
        compiler_params=pltpu.CompilerParams(
            collective_id=0, has_side_effects=True, vmem_limit_bytes=48 * 2**20
        ),
    )(signal.reshape(seg_count * chan_local, length), table, latent_factor)
    out = out.reshape(bins, 2, 2, 2, 128).transpose(0, 1, 3, 2, 4)
    return out.reshape(bins, channels // n, 2, channels)


def solution(mesh):
    in_specs = (P("seg", "chan", None), P())
    out_specs = P(None, ("seg", "chan"), None, None)
    return jax.shard_map(
        per_device, mesh=mesh, in_specs=in_specs, out_specs=out_specs, check_vma=False
    )
```

time: 370 us -> 44.9 us (0.12)
  waiting for transfers between devices: 209 us -> 0 us
  matrix products: 45 us -> 0 us
  Pallas kernels: 0 us -> 40.7 us
  other arithmetic: 32.9 us -> 0 us
  local copies, waits for them, and re-layouts: 36 us -> 3.95 us
  blocking collectives: 23.9 us -> 0 us
  between operations: 14.2 us -> 0.01 us
  starting transfers between devices: 8.41 us -> 0 us
    unnamed x2 -> x0, waiting for transfers between devices: 192 us -> none
    dot_general x7 -> x0, matrix products: 45 us -> none  [the longest x1 13.9 us: cross_terms(): jnp.einsum('fsc,fsd->fcd', imag_part, imag_part, preferred_element_type=j...]
    pallas_call x0 -> x1, Pallas kernels: none -> 40.7 us  [per_device(): pl.pallas_call(functools.partial(kernel, n_seg, n_chan, seg_count * n_seg...]
    all_to_all x1 -> x0, blocking collectives: 23.9 us -> none  [per_device(): lax.all_to_all(spectra, 'chan', split_axis=0, concat_axis=3, tiled=True)]
    another operation x1 -> x0, other arithmetic: 17.7 us -> none
    all_to_all x1 -> x0, waiting for transfers between devices: 17.3 us -> none  [per_device(): lax.all_to_all(owned.astype(jnp.bfloat16), ('seg', 'chan'), split_axis=1,...]
    convert_element_type x1 -> x0, other arithmetic: 15.1 us -> none  [per_device(): cross_terms(banded, segs).astype(jnp.bfloat16)]
    unnamed x14 -> x5, local copies, waits for them, and re-layouts: 16.7 us -> 3.95 us
  transfers between devices with their start and end apart: 2 -> 0, of which waited for: 2 -> 0; matrix products, arithmetic and copies ran while one was open for 0% -> 0% of each run, Pallas kernels for 0% -> 0%
where the time goes in v1:
time: 44.9 us; the launch traced here: 44.7 us
  Pallas kernels  40.7 us (91%)
  local copies, waits for them, and re-layouts  3.95 us (9%)
    pallas_call x1, Pallas kernels, per_device(): pl.pallas_call(functools.partial(kernel, n_seg, n_chan, seg_count * n_seg...  40.7 us
    unnamed x5, local copies, waits for them, and re-layouts  3.95 us

profile of v1, /device:TPU:1, one launch (start us, length us, event | category | flops | bytes accessed | tf_op | source)
XLA Modules:
  0.0 44.7 jit_solution(7841459594096881613)
XLA Ops:
  0.0 0.0 copy-start
  0.0 1.6 %copy-done = bf16[16,32,2048]{2,1,0:T(8,128)(2,1)S(1)} copy-done((bf16[16,32,2048]{2,1,0:T(8,128)(2,1)S(1)}, bf16[16,32,2048]{2,1,0:T(8,128)(2,1)}, u32[]{:S(2)}) %copy-start) | copy-done | bytes 2097176
  1.6 0.0 copy-start.1
  1.6 1.0 %copy-done.1 = f32[512,256]{1,0:T(8,128)S(1)} copy-done((f32[512,256]{1,0:T(8,128)S(1)}, f32[512,256]{1,0:T(8,128)}, u32[]{:S(2)}) %copy-start.1) | copy-done | bytes 524312
  2.6 40.7 %shard_map.37 = f32[4096,128]{1,0:T(8,128)S(1)} custom-call(bf16[512,2048]{1,0:T(8,128)(2,1)S(1)} %bitcast.7, bf16[1024,2048]{1,0:T(8,128)(2,1)} %constant.2.clone.tab_hbm, f32[512,256]{1,0:T(8,128)S(1)} %copy-done.1), custom_call_target="tpu_custom_call" | custom-call | tf_op jit(solution)/shard_map/pallas_call | solution.py:180
  43.4 1.3 %copy.6 = f32[512,2,2,256]{3,2,1,0:T(2,128)} copy(f32[512,2,2,256]{3,2,1,0:T(2,128)S(1)} %bitcast.6) | data formatting | bytes 4194304
Async XLA Ops:
  0.0 1.6 %copy-start = (bf16[16,32,2048]{2,1,0:T(8,128)(2,1)S(1)}, bf16[16,32,2048]{2,1,0:T(8,128)(2,1)}, u32[]{:S(2)}) copy-start(bf16[16,32,2048]{2,1,0:T(8,128)(2,1)} %param.3) | copy-start | bytes 6291460
  1.6 1.0 %copy-start.1 = (f32[512,256]{1,0:T(8,128)S(1)}, f32[512,256]{1,0:T(8,128)}, u32[]{:S(2)}) copy-start(f32[512,256]{1,0:T(8,128)} %lat_hbm.1) | copy-start | bytes 1572868

commit v2 on v1

--- a/solution.py
+++ b/solution.py
@@ -1,4 +1,5 @@
 import functools
+import random
 
 import jax
 import jax.numpy as jnp
@@ -11,7 +12,14 @@
 
 MESH = pl.DeviceIdType.MESH
 HALVES = 2
+SIDE = 4
 NT = (((1,), (1,)), ((), ()))
+
+
+def far_first():
+    steps = [(z, y, x, c) for x in range(SIDE) for y in range(SIDE) for z in range(SIDE) for c in range(2)][1:]
+    random.Random(1).shuffle(steps)
+    return sorted(steps, key=lambda step: -sum(min(v, SIDE - v) for v in step[:3]))
 
 
 def dft_rows(length, bins, devices):
@@ -50,21 +58,22 @@
     lat_in = pltpu.make_async_copy(lat_hbm, lat, in_sem.at[3])
     lat_in.start()
 
-    def coords(d):
-        return lax.div(d, n_chan), lax.rem(d, n_chan)
+    core, my_z = lax.rem(seg, 2), lax.rem(chan, SIDE)
+    my_x = lax.rem(lax.div(seg, 2), SIDE)
+    my_y = 2 * lax.div(chan, SIDE) + lax.div(seg, 2 * SIDE)
+    steps = far_first()
+
+    def coords(dz, dy, dx, dc):
+        to_y = lax.rem(my_y + dy, SIDE)
+        to_seg = 2 * SIDE * lax.rem(to_y, 2) + 2 * lax.rem(my_x + dx, SIDE) + lax.rem(core + dc, 2)
+        return to_seg, SIDE * lax.div(to_y, 2) + lax.rem(my_z + dz, SIDE)
 
     barrier = pltpu.get_barrier_semaphore()
-
-    def greet(s, carry):
-        pl.semaphore_signal(
-            barrier, inc=1, device_id=coords(lax.rem(me + s, n)), device_id_type=MESH
-        )
-        return carry
-
-    lax.fori_loop(1, n, greet, 0)
+    for step in steps:
+        pl.semaphore_signal(barrier, inc=1, device_id=coords(*step), device_id_type=MESH)
 
     def transform(h):
-        step = 128
+        step = half_rows
         low = lax.broadcasted_iota(jnp.int32, (step, 128), 0) % 8 < 4
 
         def block(i, carry):
@@ -84,18 +93,16 @@
             send1[h, pl.ds(i * 2 * pairs, 2 * pairs)] = block.astype(jnp.bfloat16)
             return carry
 
-        lax.fori_loop(0, half_rows // step, block, 0)
+        block(0, 0)
 
     def send(k, src, dst, at):
-        def one(s, carry):
-            d = lax.rem(me + s, n)
+        for step in steps:
+            to_seg, to_chan = coords(*step)
             pltpu.make_async_remote_copy(
-                src_ref=src.at[d], dst_ref=dst.at[at], send_sem=send_sem.at[k],
-                recv_sem=recv_sem.at[k], device_id=coords(d), device_id_type=MESH,
+                src_ref=src.at[to_seg * n_chan + to_chan], dst_ref=dst.at[at],
+                send_sem=send_sem.at[k], recv_sem=recv_sem.at[k],
+                device_id=(to_seg, to_chan), device_id_type=MESH,
             ).start()
-            return carry
-
-        lax.fori_loop(1, n, one, 0)
         pltpu.make_async_copy(src.at[me], dst.at[at], recv_sem.at[k]).start()
 
     def arrived(k, src, dst):
@@ -180,7 +187,7 @@
     out = pl.pallas_call(
         functools.partial(kernel, n_seg, n_chan, seg_count * n_seg),
         out_shape=jax.ShapeDtypeStruct((bins * 8, 128), f32),
-        in_specs=[pl.BlockSpec(memory_space=pl.ANY)] * 3,
+        in_specs=[pl.BlockSpec(memory_space=pltpu.HBM)] * 3,
         out_specs=pl.BlockSpec(memory_space=pltpu.VMEM),
         scratch_shapes=[
             pltpu.VMEM((seg_count * chan_local, length), bf16),
@@ -202,7 +209,7 @@
         compiler_params=pltpu.CompilerParams(
             collective_id=0, has_side_effects=True, vmem_limit_bytes=48 * 2**20
         ),
-    )(signal.reshape(seg_count * chan_local, length), table, latent_factor)
+    )(pltpu.with_memory_space_constraint(signal.reshape(seg_count * chan_local, length), pltpu.HBM), table, pltpu.with_memory_space_constraint(latent_factor, pltpu.HBM))
     out = out.reshape(bins, 2, 2, 2, 128).transpose(0, 1, 3, 2, 4)
     return out.reshape(bins, channels // n, 2, channels)
 

time: 44.9 us -> 40 us (0.89)
  local copies, waits for them, and re-layouts: 3.95 us -> 1.32 us
  Pallas kernels: 40.7 us -> 38.6 us
    unnamed x5 -> x1, local copies, waits for them, and re-layouts: 3.95 us -> 1.32 us
    pallas_call x1, Pallas kernels: 40.7 us -> 38.6 us  [per_device(): pl.pallas_call(functools.partial(kernel, n_seg, n_chan, seg_count * n_seg...]
where the time goes in v2:
time: 40 us; the launch traced here: 39.9 us
  Pallas kernels  38.6 us (96%)
  local copies, waits for them, and re-layouts  1.32 us (3%)
    pallas_call x1, Pallas kernels, per_device(): pl.pallas_call(functools.partial(kernel, n_seg, n_chan, seg_count * n_seg...  38.6 us
    unnamed x1, local copies, waits for them, and re-layouts  1.32 us

profile of v2, /device:TPU:1, one launch (start us, length us, event | category | flops | bytes accessed | tf_op | source)
XLA Modules:
  0.0 39.9 jit_solution(8844569873909238796)
XLA Ops:
  0.0 38.6 %shard_map.37 = f32[4096,128]{1,0:T(8,128)S(1)} custom-call(bf16[512,2048]{1,0:T(8,128)(2,1)} %bitcast.7, bf16[1024,2048]{1,0:T(8,128)(2,1)} %constant.2.clone.tab_hbm, f32[512,256]{1,0:T(8,128)} %lat_hbm.1), custom_call_target="tpu_custom_call" | custom-call | tf_op jit(solution)/shard_map/pallas_call | solution.py:187
  38.6 1.3 %copy.6 = f32[512,2,2,256]{3,2,1,0:T(2,128)} copy(f32[512,2,2,256]{3,2,1,0:T(2,128)S(1)} %bitcast.6) | data formatting | bytes 4194304

commit v3 on v2

--- a/solution.py
+++ b/solution.py
@@ -1,4 +1,5 @@
 import functools
+import itertools
 import random
 
 import jax
@@ -54,9 +55,8 @@
     for h in range(HALVES):
         rows = pl.ds(h * half_rows, half_rows)
         tab_in.append(pltpu.make_async_copy(tab_hbm.at[rows], tab.at[rows], in_sem.at[1 + h]))
-        tab_in[-1].start()
     lat_in = pltpu.make_async_copy(lat_hbm, lat, in_sem.at[3])
-    lat_in.start()
+    tab_in[0].start()
 
     core, my_z = lax.rem(seg, 2), lax.rem(chan, SIDE)
     my_x = lax.rem(lax.div(seg, 2), SIDE)
@@ -69,31 +69,26 @@
         return to_seg, SIDE * lax.div(to_y, 2) + lax.rem(my_z + dz, SIDE)
 
     barrier = pltpu.get_barrier_semaphore()
-    for step in steps:
+    for step in itertools.product((2, 1, 3, 0), (2, 1, 3, 0), (2, 1, 3, 0), (1, 0)):
+        if not any(step):
+            continue
         pl.semaphore_signal(barrier, inc=1, device_id=coords(*step), device_id_type=MESH)
+    tab_in[1].start()
+    lat_in.start()
 
     def transform(h):
-        step = half_rows
-        low = lax.broadcasted_iota(jnp.int32, (step, 128), 0) % 8 < 4
-
-        def block(i, carry):
-            rows = pl.ds(pl.multiple_of(h * half_rows + i * step, step), step)
-            y = lax.dot_general(tab[rows, :], sig[...], NT, preferred_element_type=jnp.float32)
-            v = [y[:, q * 128 : (q + 1) * 128] for q in range(4)]
-            up = [pltpu.roll(a, 4, 0) for a in v]
-            even = [jnp.where(low, v[q], up[q + 1]) for q in (0, 2)]
-            down = [pltpu.roll(a, step - 4, 0) for a in v]
-            odd = [jnp.where(low, down[q], v[q + 1]) for q in (0, 2)]
-            pairs = step // 8
-            both = [
-                jnp.concatenate([a.reshape(pairs, 1, 8, 128) for a in part], axis=2)
-                for part in (even, odd)
-            ]
-            block = jnp.concatenate(both, axis=1).reshape(2 * pairs, 16, 128)
-            send1[h, pl.ds(i * 2 * pairs, 2 * pairs)] = block.astype(jnp.bfloat16)
-            return carry
-
-        block(0, 0)
+        low = lax.broadcasted_iota(jnp.int32, (half_rows, 128), 0) % 8 < 4
+        rows = pl.ds(h * half_rows, half_rows)
+        y = lax.dot_general(tab[rows, :], sig[...], NT, preferred_element_type=jnp.float32)
+        v = [y[:, q * 128 : (q + 1) * 128] for q in range(4)]
+        even = [jnp.where(low, v[q], pltpu.roll(v[q + 1], 4, 0)) for q in (0, 2)]
+        odd = [jnp.where(low, pltpu.roll(v[q], half_rows - 4, 0), v[q + 1]) for q in (0, 2)]
+        pairs = half_rows // 8
+        both = [
+            jnp.concatenate([a.reshape(pairs, 1, 8, 128) for a in part], axis=2)
+            for part in (even, odd)
+        ]
+        send1[h] = jnp.concatenate(both, axis=1).reshape(n, 16, 128).astype(jnp.bfloat16)
 
     def send(k, src, dst, at):
         for step in steps:
@@ -133,21 +128,26 @@
         left = pl.ds(h * 2 * n, 2 * n)
         for c in range(2):
             for dh in range(2):
-                for k in range(2):
-                    at = c * 4 + dh * 2 + k
-                    x = jnp.concatenate(
+                cols = [
+                    jnp.concatenate(
                         [
                             scr[pl.ds(c * 8 + b * 4 + k * 2 + dh, n, stride=16), :]
                             for b in range(2)
                         ],
                         axis=0,
                     ).astype(jnp.bfloat16)
-                    r = jnp.dot(m_hi[:, left], x, preferred_element_type=jnp.float32)
-                    r = r + jnp.dot(m_lo[:, left], x, preferred_element_type=jnp.float32)
+                    for k in range(2)
+                ]
+                x = jnp.concatenate(cols, axis=1)
+                r = jnp.dot(m_hi[:, left], x, preferred_element_type=jnp.float32)
+                r = r + jnp.dot(m_lo[:, left], x, preferred_element_type=jnp.float32)
+                for k in range(2):
+                    at = c * 4 + dh * 2 + k
+                    part = r[:, k * 128 : (k + 1) * 128]
                     if h == 0:
-                        acc[at] = r
+                        acc[at] = part
                     else:
-                        out_ref[pl.ds(at, bins, stride=8), :] = r + acc[at]
+                        out_ref[pl.ds(at, bins, stride=8), :] = part + acc[at]
 
     sig_in.wait()
     tab_in[0].wait()

time: 40 us -> 38.3 us (0.957)
  Pallas kernels: 38.6 us -> 36.8 us
    pallas_call x1, Pallas kernels: 38.6 us -> 36.8 us  [per_device(): pl.pallas_call(functools.partial(kernel, n_seg, n_chan, seg_count * n_seg...]
where the time goes in v3:
time: 38.3 us; the launch traced here: 38.2 us
  Pallas kernels  36.8 us (96%)
  local copies, waits for them, and re-layouts  1.32 us (3%)
    pallas_call x1, Pallas kernels, per_device(): pl.pallas_call(functools.partial(kernel, n_seg, n_chan, seg_count * n_seg...  36.8 us
    unnamed x1, local copies, waits for them, and re-layouts  1.32 us

profile of v3, /device:TPU:1, one launch (start us, length us, event | category | flops | bytes accessed | tf_op | source)
XLA Modules:
  0.0 38.2 jit_solution(10749888334452350119)
XLA Ops:
  0.0 36.8 %shard_map.37 = f32[4096,128]{1,0:T(8,128)S(1)} custom-call(bf16[512,2048]{1,0:T(8,128)(2,1)} %bitcast.7, bf16[1024,2048]{1,0:T(8,128)(2,1)} %constant.2.clone.tab_hbm, f32[512,256]{1,0:T(8,128)} %lat_hbm.1), custom_call_target="tpu_custom_call" | custom-call | tf_op jit(solution)/shard_map/pallas_call | solution.py:187
  36.8 1.3 %copy.6 = f32[512,2,2,256]{3,2,1,0:T(2,128)} copy(f32[512,2,2,256]{3,2,1,0:T(2,128)S(1)} %bitcast.6) | data formatting | bytes 4194304

commit v4 on v3

--- a/solution.py
+++ b/solution.py
@@ -167,12 +167,16 @@
         arrived(h, send1.at[h], recv1.at[h])
         cross(h)
         send(2 + h, send2.at[h], recv2.at[h], me)
+    def sent(k):
+        src = (send1, send2)[k // HALVES].at[k % HALVES, pl.ds(0, n - 1)]
+        pltpu.make_async_copy(src, src, send_sem.at[k]).wait()
+
     for h in range(HALVES):
+        if h == HALVES - 1:
+            for k in range(2 * HALVES):
+                sent(k)
         arrived(2 + h, send2.at[h], recv2.at[h])
         smooth(h)
-    for k in range(2 * HALVES):
-        src = (send1, send2)[k // HALVES].at[k % HALVES, pl.ds(0, n - 1)]
-        pltpu.make_async_copy(src, src, send_sem.at[k]).wait()
 
 
 def per_device(signal, latent_factor):

time: 38.3 us -> 38.3 us (level)
  no operation moved by 1% of the time
where the time goes in v4:
time: 38.3 us; the launch traced here: 38.2 us
  Pallas kernels  36.8 us (96%)
  local copies, waits for them, and re-layouts  1.32 us (3%)
    pallas_call x1, Pallas kernels, per_device(): pl.pallas_call(functools.partial(kernel, n_seg, n_chan, seg_count * n_seg...  36.8 us
    unnamed x1, local copies, waits for them, and re-layouts  1.32 us

profile of v4, /device:TPU:1, one launch (start us, length us, event | category | flops | bytes accessed | tf_op | source)
XLA Modules:
  0.0 38.2 jit_solution(7179096246183224510)
XLA Ops:
  0.0 36.8 %shard_map.37 = f32[4096,128]{1,0:T(8,128)S(1)} custom-call(bf16[512,2048]{1,0:T(8,128)(2,1)} %bitcast.7, bf16[1024,2048]{1,0:T(8,128)(2,1)} %constant.2.clone.tab_hbm, f32[512,256]{1,0:T(8,128)} %lat_hbm.1), custom_call_target="tpu_custom_call" | custom-call | tf_op jit(solution)/shard_map/pallas_call | solution.py:191
  36.8 1.3 %copy.6 = f32[512,2,2,256]{3,2,1,0:T(2,128)} copy(f32[512,2,2,256]{3,2,1,0:T(2,128)S(1)} %bitcast.6) | data formatting | bytes 4194304

commit v5 on v4

--- a/solution.py
+++ b/solution.py
@@ -91,6 +91,7 @@
         send1[h] = jnp.concatenate(both, axis=1).reshape(n, 16, 128).astype(jnp.bfloat16)
 
     def send(k, src, dst, at):
+        pltpu.make_async_copy(src.at[me], dst.at[at], recv_sem.at[k]).start()
         for step in steps:
             to_seg, to_chan = coords(*step)
             pltpu.make_async_remote_copy(
@@ -98,7 +99,6 @@
                 send_sem=send_sem.at[k], recv_sem=recv_sem.at[k],
                 device_id=(to_seg, to_chan), device_id_type=MESH,
             ).start()
-        pltpu.make_async_copy(src.at[me], dst.at[at], recv_sem.at[k]).start()
 
     def arrived(k, src, dst):
         pltpu.make_async_copy(src, dst, recv_sem.at[k]).wait()

time: 38.3 us -> 38.3 us (level)
  no operation moved by 1% of the time
where the time goes in v5:
time: 38.3 us; the launch traced here: 38.2 us
  Pallas kernels  36.9 us (96%)
  local copies, waits for them, and re-layouts  1.32 us (3%)
    pallas_call x1, Pallas kernels, per_device(): pl.pallas_call(functools.partial(kernel, n_seg, n_chan, seg_count * n_seg...  36.9 us
    unnamed x1, local copies, waits for them, and re-layouts  1.32 us

profile of v5, /device:TPU:1, one launch (start us, length us, event | category | flops | bytes accessed | tf_op | source)
XLA Modules:
  0.0 38.2 jit_solution(7208966467676355180)
XLA Ops:
  0.0 36.9 %shard_map.37 = f32[4096,128]{1,0:T(8,128)S(1)} custom-call(bf16[512,2048]{1,0:T(8,128)(2,1)} %bitcast.7, bf16[1024,2048]{1,0:T(8,128)(2,1)} %constant.2.clone.tab_hbm, f32[512,256]{1,0:T(8,128)} %lat_hbm.1), custom_call_target="tpu_custom_call" | custom-call | tf_op jit(solution)/shard_map/pallas_call | solution.py:191
  36.9 1.3 %copy.6 = f32[512,2,2,256]{3,2,1,0:T(2,128)} copy(f32[512,2,2,256]{3,2,1,0:T(2,128)S(1)} %bitcast.6) | data formatting | bytes 4194304
